TPU v7x, 128 devices: a whole 4x4x4 slice. The times are simulated.
128 devices in a mesh: row: 8 (over z, x_hi), col: 16 (over x_lo, y, core).
Axes of the slice: x: 4 (x_hi: 2, x_lo: 2; x = x_hi * 2 + x_lo), y: 4, z: 4, core: 2. Of those that a mesh axis runs over, the one named last changes fastest.
Arguments:
- cycle_cells: int32 [2, 16384], P(None, ('row', 'col')), may hold values from 0 to 1023, as said below
- cycle_offsets: float32 [2, 16384], P(None, ('row', 'col')), may hold values from 0 to 1
- cycle_strength: float32 [16384], P(('row', 'col')), may hold values from -48 to 48
- block_tile: int32 [8192], P(('row', 'col')), may hold values from 0 to 127, as said below
Outputs:
- displacement: float32 [2, 16384], P(None, ('row', 'col'))
- diffused: float32 [4096, 8192], P('col', 'row')
- renewed: float32 [16384], P(('row', 'col'))
Inputs may be any that keep to these rules, and one draw needn't show every extreme that they name: Block b's cycles lie in the tile with slab block_tile[b] // 16 and radial part block_tile[b] mod 16. The blocks of one device name one tile at most 2 times and one slab at most 2 * 16 times; in every draw some slab is named 2 * 16 times by every device, each of its tiles twice. `cycle_cells`: row 0 is a radial cell within the cycle's tile, below 256; row 1 an axial cell, below 1024.
All inputs are finite; a program needn't handle non-finite values.
Results may differ from a plain program's by a relative error of at most 0.0004.
Values sent between devices are 32-bit elements; how exact they have to be, the bound alone decides.
A program may use at most 64 MiB of HBM per device.

v0:
```python
import math
import jax
import jax.numpy as jnp
from jax import lax
from jax.sharding import PartitionSpec as P

CR = 256
CZ = 1024
AGM_STEPS = 6
CORE_SQUARE = 4.0
STEP_LENGTH = 4.0
VISCOSITY = 0.2


def passed_along(block, axis, distance):
    devices = range(lax.axis_size(axis))
    route = [(i - distance, i) for i in devices if i - distance in devices]
    return lax.ppermute(block, axis, route)


def extended(shard, sides, width):
    for axis, dim in sides:
        peers, length = (lax.axis_size(axis), shard.shape[dim])
        up = [(i, (i + 1) % peers) for i in range(peers - 1)]
        down = [(j, i) for i, j in up]
        last = lax.slice_in_dim(shard, length - width, length, axis=dim)
        first = lax.slice_in_dim(shard, 0, width, axis=dim)
        before = lax.ppermute(last, axis, up)
        after = lax.ppermute(first, axis, down)
        shard = jnp.concatenate([before, shard, after], axis=dim)
    return shard


def tent_weight(distance):
    return jnp.maximum(1.0 - jnp.abs(distance), 0.0)


def pair_sums(targets, sources):
    target_r = targets[0][:, None]
    target_z = targets[1][:, None]
    source_r = sources[0][None, :]
    source_z = sources[1][None, :]
    source_gamma = sources[2][None, :]
    axial_gap = target_z - source_z
    smooth_sq = axial_gap * axial_gap + CORE_SQUARE
    radius_sum = target_r + source_r
    radius_gap = target_r - source_r
    far_sq = radius_sum * radius_sum + smooth_sq
    near_sq = radius_gap * radius_gap + smooth_sq
    modulus_sq = 4.0 * target_r * source_r / far_sq
    upper_mean = jnp.ones_like(far_sq)
    lower_mean = jnp.sqrt(near_sq / far_sq)
    series = 0.5 * modulus_sq
    factor = 1.0
    for agm_step in range(AGM_STEPS):
        half_gap = 0.5 * (upper_mean - lower_mean)
        upper_mean, lower_mean = (
            0.5 * (upper_mean + lower_mean),
            jnp.sqrt(upper_mean * lower_mean),
        )
        series = series + factor * half_gap * half_gap
        factor = factor * 2.0
    kind_first = 0.5 * math.pi / upper_mean
    kind_second = kind_first * (1.0 - series)
    prefactor = source_gamma / (2.0 * math.pi * jnp.sqrt(far_sq))
    square_sum = source_r * source_r + target_r * target_r + smooth_sq
    square_gap = source_r * source_r - target_r * target_r - smooth_sq
    axial_part = prefactor * (kind_first + square_gap / near_sq * kind_second)
    radial_part = (
        prefactor * axial_gap / target_r * (square_sum / near_sq * kind_second - kind_first)
    )
    return jnp.stack([jnp.sum(radial_part, axis=1), jnp.sum(axial_part, axis=1)])


def cycle_velocity(targets, sources):
    target_count = targets.shape[1]
    block_width = 512
    grouped = targets.reshape(2, target_count // block_width, block_width).transpose(1, 0, 2)
    result = lax.map(lambda target_group: pair_sums(target_group, sources), grouped)
    return result.transpose(1, 0, 2).reshape(2, target_count)


def diffuse(padded, first_row):
    center = padded[1:-1, 1:-1]
    outward = padded[2:, 1:-1]
    inward = padded[:-2, 1:-1]
    forward_z = padded[1:-1, 2:]
    backward_z = padded[1:-1, :-2]
    radius = jnp.maximum(first_row + jnp.arange(center.shape[0], dtype=jnp.int32), 1).astype(
        jnp.float32
    )[:, None]
    laplace = (
        outward
        + inward
        + forward_z
        + backward_z
        - 4.0 * center
        + (outward - inward) / (2.0 * radius)
        - center / (radius * radius)
    )
    return center + VISCOSITY * laplace


def rank_slots(group_of_block, capacity, per_block):
    block_count = group_of_block.shape[0]
    numbering = jnp.arange(block_count, dtype=jnp.int32)
    earlier = (group_of_block[:, None] == group_of_block[None, :]) & (
        numbering[None, :] < numbering[:, None]
    )
    standing = jnp.sum(earlier.astype(jnp.int32), axis=1)
    first_slot = (group_of_block * capacity + standing) * per_block
    return (first_slot[:, None] + jnp.arange(per_block, dtype=jnp.int32)[None, :]).reshape(-1)


def slot_matrix(cycle_slot, slot_total):
    return (jnp.arange(slot_total, dtype=jnp.int32)[None, :] == cycle_slot[:, None]).astype(
        jnp.float32
    )


def cycle_weights(cell, offset, anchor, total):
    grid_at = anchor + jnp.arange(total, dtype=jnp.int32)
    delta = (grid_at[:, None] - cell[None, :]).astype(jnp.float32)
    return tent_weight(offset[None, :] - delta)


def deposit_cycles(arrived, row_anchor, row_total, col_anchor, col_total):
    cycle_r = arrived[0].astype(jnp.int32)
    cycle_z = arrived[1].astype(jnp.int32)
    radial_weights = cycle_weights(cycle_r, arrived[2], row_anchor, row_total) * arrived[4][None, :]
    axial_weights = cycle_weights(cycle_z, arrived[3], col_anchor, col_total)
    return lax.dot_general(
        radial_weights,
        axial_weights,
        (((1,), (1,)), ((), ())),
        precision=lax.Precision.HIGHEST,
        preferred_element_type=jnp.float32,
    )


def sample_field(field_part, arrived, row_anchor, col_anchor):
    cycle_r = arrived[0].astype(jnp.int32)
    cycle_z = arrived[1].astype(jnp.int32)
    radial_weights = cycle_weights(cycle_r, arrived[2], row_anchor, field_part.shape[0])
    axial_weights = cycle_weights(cycle_z, arrived[3], col_anchor, field_part.shape[1])
    along_rows = jnp.dot(
        field_part,
        axial_weights,
        precision=lax.Precision.HIGHEST,
        preferred_element_type=jnp.float32,
    )
    return jnp.sum(radial_weights * along_rows, axis=0)


def on_device(cycle_cells, cycle_offsets, cycle_strength, block_tile):
    row_devices = lax.axis_size("row")
    col_devices = lax.axis_size("col")
    per_block = cycle_cells.shape[1] // block_tile.shape[0]
    cycle_tile = jnp.repeat(block_tile, per_block)
    cell_r = jnp.clip(cycle_tile % col_devices * CR + cycle_cells[0], 16, CR * col_devices - 3)
    cell_z = jnp.clip(cycle_tile // col_devices * CZ + cycle_cells[1], 2, CZ * row_devices - 3)
    positions = jnp.stack(
        [
            cell_r.astype(jnp.float32) + cycle_offsets[0],
            cell_z.astype(jnp.float32) + cycle_offsets[1],
        ]
    )
    own_sources = jnp.concatenate([positions, cycle_strength[None, :]], axis=0)
    row_targets = lax.all_gather(positions, "col", axis=1, tiled=True)
    partial_sums = cycle_velocity(
        row_targets, lax.all_gather(own_sources, "row", axis=1, tiled=True)
    )
    velocity = lax.psum_scatter(partial_sums, "col", scatter_dimension=1, tiled=True)
    displacement = STEP_LENGTH * velocity
    moved_offsets = jnp.clip(cycle_offsets + displacement, -1.0, 2.0)
    payload = jnp.stack(
        [
            cell_r.astype(jnp.float32),
            cell_z.astype(jnp.float32),
            moved_offsets[0],
            moved_offsets[1],
            cycle_strength,
        ]
    )
    row_start = lax.axis_index("col") * CR
    col_start = lax.axis_index("row") * CZ
    cycle_slot = rank_slots(block_tile // col_devices, 2 * col_devices, per_block)
    slot_table = slot_matrix(cycle_slot, row_devices * 2 * col_devices * per_block)
    outgoing = jnp.dot(
        payload, slot_table, precision=lax.Precision.HIGHEST, preferred_element_type=jnp.float32
    )
    arrived = lax.all_to_all(outgoing, "row", split_axis=1, concat_axis=1, tiled=True)
    folded_r = lax.psum_scatter(
        deposit_cycles(arrived, jnp.int32(0), CR * lax.axis_size("col"), col_start - 1, CZ + 3),
        "col",
        scatter_dimension=0,
        tiled=True,
    )
    from_next_z = passed_along(folded_r[:, 0:1], "row", -1)
    from_prev_z = passed_along(folded_r[:, CZ + 1 : CZ + 3], "row", 1)
    deposited = folded_r[:, 1 : CZ + 1]
    deposited = deposited.at[:, CZ - 1 : CZ].add(from_next_z)
    deposited = deposited.at[:, 0:2].add(from_prev_z)
    padded = extended(deposited, (("row", 1), ("col", 0)), 1)
    diffused = diffuse(padded, row_start)
    widened = extended(diffused, (("row", 1),), 2)
    values = sample_field(
        lax.all_gather(widened, "col", axis=0, tiled=True), arrived, jnp.int32(0), col_start - 2
    )
    returned = lax.all_to_all(values, "row", split_axis=0, concat_axis=0, tiled=True)
    renewed = jnp.dot(
        slot_table, returned, precision=lax.Precision.HIGHEST, preferred_element_type=jnp.float32
    )
    return (displacement, diffused, renewed)


def solution(mesh):
    in_specs = (
        P(None, ("row", "col")),
        P(None, ("row", "col")),
        P(("row", "col")),
        P(("row", "col")),
    )
    out_specs = (P(None, ("row", "col")), P("col", "row"), P(("row", "col")))
    return jax.shard_map(
        on_device, mesh=mesh, in_specs=in_specs, out_specs=out_specs, check_vma=False
    )
```

profile of v0, /device:TPU:0, one launch (start us, length us, event | category | flops | bytes accessed | tf_op | source)
XLA Modules:
  0.0 520.6 jit_solution(1767718619613536940)
XLA Ops:
  7.2 0.7 broadcast_in_dim.20
  8.1 0.8 slice_add_fusion.2
  8.9 0.7 pad_maximum_fusion.4
  9.6 32.1 %all_gather.9 = f32[3,1024]{1,0:T(4,128)S(1)} all-gather(f32[3,128]{1,0:T(4,128)S(1)} %pad_maximum_fusion.4), channel_id=1, replica_groups=mesh['row'=8,'col'=16] {'row'}, dimensions={1}, use_global_device_ids=true | all-gather | bytes 13824 | tf_op jit(solution)/shard_map/all_gather | solution.py:171
  41.6 19.8 %all_gather.10 = f32[2,2048]{1,0:T(2,128)S(1)} all-gather(f32[2,128]{1,0:T(2,128)S(1)} %pad_maximum_fusion.5), channel_id=1, replica_groups=mesh['row'=8,'col'=16] {'col'}, dimensions={1}, use_global_device_ids=true | all-gather | bytes 17408 | tf_op jit(solution)/shard_map/all_gather | solution.py:169
  61.5 39.3 %while.14 = (s32[]{:T(128)}, f32[4,2,512]{2,1,0:T(2,128)S(1)}, f32[3,1024]{1,0:T(4,128)S(1)}, f32[4,2,512]{2,1,0:T(2,128)S(1)}, f32[1,1024]{1,0:T(1,128)S(1)}, /*index=5*/s32[]{:T(128)}, s32[]{:T(128)}, s32[]{}) while((s32[]{:T(128)}, f32[4,2,512]{2,1,0:T(2,128)S(1)}, f32[3,1024]{1,0:T(4,128)S(1)}, f32[4,2,512]{2,1,0:T(2,128)S(1)}, ...), condition=%wide.region_3.4_spmd, body=%wide.region_0.3_spmd.sunk | while | flops 40895488 | bytes 75893 | solution.py:79
  61.5 9.7 %fusion.90 = (f32[512]{0:T(512)S(1)}, f32[512]{0:T(512)S(1)}) fusion(f32[512]{0:T(512)S(1)} %get-tuple-element.184, f32[1024]{0:T(1024)S(1)} %bitcast.64, f32[1024]{0:T(1024)S(1)} %bitcast.54, f32[512]{0:T(512)S(1)} %bitcast.62, f32[1024]{0:T(1024)S(1)} %bitcast.55, f32[512]{0:T(512)S(1)} %bitcast.51, f32[512]{0:T(512)S(1)} %get-tuple-element.188, ...), kind=kLoop, calls=%fused_computation.38.clone.1 | loop fusion | flops 40893440 | bytes 28672 | tf_op jit(solution)/shard_map/while/body/eval_jaxpr/reduce_sum | solution.py:72
  71.3 9.7 %fusion.90 = (f32[512]{0:T(512)S(1)}, f32[512]{0:T(512)S(1)}) fusion(f32[512]{0:T(512)S(1)} %get-tuple-element.184, f32[1024]{0:T(1024)S(1)} %bitcast.64, f32[1024]{0:T(1024)S(1)} %bitcast.54, f32[512]{0:T(512)S(1)} %bitcast.62, f32[1024]{0:T(1024)S(1)} %bitcast.55, f32[512]{0:T(512)S(1)} %bitcast.51, f32[512]{0:T(512)S(1)} %get-tuple-element.188, ...), kind=kLoop, calls=%fused_computation.38.clone.1 | loop fusion | flops 40893440 | bytes 28672 | tf_op jit(solution)/shard_map/while/body/eval_jaxpr/reduce_sum | solution.py:72
  81.2 9.7 %fusion.90 = (f32[512]{0:T(512)S(1)}, f32[512]{0:T(512)S(1)}) fusion(f32[512]{0:T(512)S(1)} %get-tuple-element.184, f32[1024]{0:T(1024)S(1)} %bitcast.64, f32[1024]{0:T(1024)S(1)} %bitcast.54, f32[512]{0:T(512)S(1)} %bitcast.62, f32[1024]{0:T(1024)S(1)} %bitcast.55, f32[512]{0:T(512)S(1)} %bitcast.51, f32[512]{0:T(512)S(1)} %get-tuple-element.188, ...), kind=kLoop, calls=%fused_computation.38.clone.1 | loop fusion | flops 40893440 | bytes 28672 | tf_op jit(solution)/shard_map/while/body/eval_jaxpr/reduce_sum | solution.py:72
  91.0 9.8 %fusion.90 = (f32[512]{0:T(512)S(1)}, f32[512]{0:T(512)S(1)}) fusion(f32[512]{0:T(512)S(1)} %get-tuple-element.184, f32[1024]{0:T(1024)S(1)} %bitcast.64, f32[1024]{0:T(1024)S(1)} %bitcast.54, f32[512]{0:T(512)S(1)} %bitcast.62, f32[1024]{0:T(1024)S(1)} %bitcast.55, f32[512]{0:T(512)S(1)} %bitcast.51, f32[512]{0:T(512)S(1)} %get-tuple-element.188, ...), kind=kLoop, calls=%fused_computation.38.clone.1 | loop fusion | flops 40893440 | bytes 28672 | tf_op jit(solution)/shard_map/while/body/eval_jaxpr/reduce_sum | solution.py:72
  100.8 1.3 copy.31
  102.7 57.9 %reduce-scatter.7.cloned.1.call-done = f32[128,2]{1,0:T(8,128)} async-done(((f32[2048,2]{1,0:T(8,128)}), f32[128,2]{1,0:T(8,128)}) %reduce-scatter.7.cloned.1.call-update) | async-done | bytes 1040
  160.6 0.9 copy.32
  162.4 0.7 reshape.303
  163.1 6.6 %all-to-all-start = ((f32[8,1,320]{2,1,0:T(1,128)}), f32[8,1,320]{2,1,0:T(1,128)S(1)}, u32[]{:S(2)}, u32[]{:S(2)}) async-start(f32[8,1,320]{2,1,0:T(1,128)} %reshape.303), calls=%async_computation | async-start | bytes 24576 | tf_op jit(solution)/shard_map/all_to_all | solution.py:192
  169.9 7.5 %all-to-all-done = f32[8,1,320]{2,1,0:T(1,128)S(1)} async-done(((f32[8,1,320]{2,1,0:T(1,128)}), f32[8,1,320]{2,1,0:T(1,128)S(1)}, u32[]{:S(2)}, u32[]{:S(2)}) %all-to-all-start) | async-done | bytes 10272 | tf_op jit(solution)/shard_map/all_to_all | solution.py:192
  177.9 0.7 reduce.34
  179.1 37.6 %fusion.25 = f32[4096,1027]{0,1:T(8,128)} fusion(f32[512]{0:T(512)S(1)} %mul.386, s32[512]{0:T(512)S(1)} %convert_element_type.62, f32[512]{0:T(512)S(1)} %sub.233, s32[512]{0:T(512)S(1)} %convert_element_type.65, s32[1027]{0:T(1024)S(1)} %iota_add_fusion.2, f32[512]{0:T(512)S(1)} %sub.241), kind=kOutput, calls=%fused_computation.45 | convolution fusion | flops 25863135232 | bytes 16840716 | tf_op jit(solution)/shard_map/dot_general | solution.py:132
  216.7 93.5 %reduce-scatter.5.cloned.1.call-done = f32[256,1027]{0,1:T(8,128)} async-done(((f32[4096,1027]{0,1:T(8,128)}), f32[256,1027]{0,1:T(8,128)}) %reduce-scatter.5.cloned.1.call-update) | async-done | bytes 1051664 | tf_op jit(solution)/shard_map/reduce_scatter | solution.py:193
  310.2 0.7 slice.190
  310.9 1.3 collective-permute-start
  312.9 0.7 slice.192
  313.6 6.0 %collective-permute-start.1 = (f32[256,2]{0,1:T(2,128)S(1)}, f32[256,2]{0,1:T(2,128)S(1)}, u32[]{:S(2)}, u32[]{:S(2)}) collective-permute-start(f32[256,2]{0,1:T(2,128)S(1)} %slice.192), channel_id=1, source_target_pairs={{0,16},{16,32},{32,48},{48,64},{64,80},{80,96},{96,112},{1,17},{17... | collective-permute-start | bytes 6152 | tf_op jit(solution)/shard_map/ppermute | solution.py:18
  319.6 1.3 slice.188
  320.9 0.7 slice_add_fusion
  322.3 5.5 %collective-permute-start.2 = (f32[256,1]{0,1:T(1,128)S(1)}, f32[256,1]{0,1:T(1,128)S(1)}, u32[]{:S(2)}, u32[]{:S(2)}) collective-permute-start(f32[256,1]{0,1:T(1,128)S(1)} %slice.193), channel_id=1, source_target_pairs={{0,16},{16,32},{32,48},{48,64},{64,80},{80,96},{96,112},{1,17},{17... | collective-permute-start | bytes 3080 | tf_op jit(solution)/shard_map/ppermute | solution.py:28
  327.8 1.3 collective-permute-start.3
  329.2 6.1 %collective-permute-done.3 = f32[256,1]{0,1:T(1,128)S(1)} collective-permute-done((f32[256,1]{0,1:T(1,128)S(1)}, f32[256,1]{0,1:T(1,128)S(1)}, u32[]{:S(2)}, u32[]{:S(2)}) %collective-permute-start.3) | collective-permute-done | bytes 1056 | tf_op jit(solution)/shard_map/ppermute | solution.py:29
  335.2 0.9 concatenate.28
  336.1 0.9 fusion.82
  337.1 1.2 copy.25
  338.3 1.3 collective-permute-start.4
  339.8 3.0 collective-permute-start.5
  342.9 1.0 copy.26
  343.9 1.0 copy.28
  345.0 2.2 fusion.59
  347.2 6.3 %collective-permute-start.6 = (f32[256,2]{0,1:T(2,128)S(1)}, f32[256,2]{0,1:T(2,128)S(1)}, u32[]{:S(2)}, u32[]{:S(2)}) collective-permute-start(f32[256,2]{0,1:T(2,128)S(1)} %get-tuple-element.138), channel_id=1, source_target_pairs={{0,16},{16,32},{32,48},{48,64},{64,80},{80,96},{96,112},{1,17},{17... | collective-permute-start | bytes 6152 | tf_op jit(solution)/shard_map/ppermute | solution.py:28
  353.5 1.3 collective-permute-start.7
  354.8 5.7 %collective-permute-done.7 = f32[256,2]{0,1:T(2,128)S(1)} collective-permute-done((f32[256,2]{0,1:T(2,128)S(1)}, f32[256,2]{0,1:T(2,128)S(1)}, u32[]{:S(2)}, u32[]{:S(2)}) %collective-permute-start.7) | collective-permute-done | bytes 2080 | tf_op jit(solution)/shard_map/ppermute | solution.py:29
  360.5 4.9 concatenate.33
  365.4 92.0 %all-gather.2.cloned.1.call-done = f32[4096,1028]{0,1:T(8,128)} async-done(((f32[256,1028]{0,1:T(8,128)}), f32[4096,1028]{0,1:T(8,128)}) %all-gather.2.cloned.1.call-update) | async-done | bytes 16842768 | tf_op jit(solution)/shard_map/all_gather | solution.py:208
  457.4 39.4 %multiply_reduce_fusion = f32[512]{0:T(512)S(1)} fusion(f32[4096,1028]{0,1:T(8,128)} %all-gather.2.cloned.1.call-done, s32[512]{0:T(512)S(1)} %convert_element_type.62, f32[512]{0:T(512)S(1)} %sub.233, s32[512]{0:T(512)S(1)} %convert_element_type.65, s32[1028]{0:T(1024)S(1)} %iota_add_fusion.1, f32[512]{0:T(512)S(1)} %sub.241), kind=kOutput, calls=%fused_computation.44 | convolution fusion | flops 25890402304 | bytes 16857104 | tf_op jit(solution)/shard_map/dot_general | solution.py:146
  496.9 0.7 all_to_all.16
  497.5 6.8 %all-to-all-start.1 = ((f32[8,64,1]{1,2,0:T(1,128)}), f32[8,64,1]{1,2,0:T(1,128)S(1)}, u32[]{:S(2)}, u32[]{:S(2)}) async-start(f32[8,64,1]{1,2,0:T(1,128)} %bitcast.14), calls=%async_computation.2 | async-start | bytes 8192 | tf_op jit(solution)/shard_map/all_to_all | solution.py:210
  504.4 1.3 copy.30
  505.7 6.4 %all-to-all-done.1 = f32[8,64,1]{1,2,0:T(1,128)S(1)} async-done(((f32[8,64,1]{1,2,0:T(1,128)}), f32[8,64,1]{1,2,0:T(1,128)S(1)}, u32[]{:S(2)}, u32[]{:S(2)}) %all-to-all-start.1) | async-done | bytes 2080 | tf_op jit(solution)/shard_map/all_to_all | solution.py:210
  512.5 0.7 reduce.33
  513.3 0.8 convolution_bitcast_fusion
  (68 shorter events, 5.2 us)
Async XLA Ops:
  7.2 153.4 %reduce-scatter.7.cloned.1.call-start = ((), (), s32[]{:S(2)}) async-start(), calls=%async_computation.6 | async-start | bytes 1114112
  100.8 1.4 copy-start.1
  100.8 60.6 %copy-start = (f32[2,128]{1,0:T(2,128)S(1)}, f32[2,128]{1,0:T(2,128)}, u32[]{:S(2)}) copy-start(f32[2,128]{1,0:T(2,128)} %param.11) | copy-start | bytes 3076
  100.8 61.2 %copy-start.2 = (f32[128]{0:T(128)S(1)}, f32[128]{0:T(128)}, u32[]{:S(2)}) copy-start(f32[128]{0:T(128)} %param.12) | copy-start | bytes 1540
  163.1 14.3 %all-to-all-start = ((f32[8,1,320]{2,1,0:T(1,128)}), f32[8,1,320]{2,1,0:T(1,128)S(1)}, u32[]{:S(2)}, u32[]{:S(2)}) async-start(f32[8,1,320]{2,1,0:T(1,128)} %reshape.303), calls=%async_computation | async-start | bytes 24576 | tf_op jit(solution)/shard_map/all_to_all | solution.py:192
  169.6 140.6 %reduce-scatter.5.cloned.1.call-start = ((), (), s32[]{:S(2)}) async-start(), calls=%async_computation.4 | async-start | bytes 17965056 | tf_op jit(solution)/shard_map/reduce_scatter | solution.py:193
  216.7 240.7 %all-gather.2.cloned.1.call-start = ((), (), s32[]{:S(2)}) async-start(), calls=%async_computation.5 | async-start | bytes 17965056 | tf_op jit(solution)/shard_map/all_gather | solution.py:208
  310.9 10.0 %collective-permute-start = (f32[256,1]{0,1:T(1,128)S(1)}, f32[256,1]{0,1:T(1,128)S(1)}, u32[]{:S(2)}, u32[]{:S(2)}) collective-permute-start(f32[256,1]{0,1:T(1,128)S(1)} %slice.190), channel_id=1, source_target_pairs={{16,0},{32,16},{48,32},{64,48},{80,64},{96,80},{112,96},{17,1},{33... | collective-permute-start | bytes 3080 | tf_op jit(solution)/shard_map/ppermute | solution.py:18
  313.6 8.1 %collective-permute-start.1 = (f32[256,2]{0,1:T(2,128)S(1)}, f32[256,2]{0,1:T(2,128)S(1)}, u32[]{:S(2)}, u32[]{:S(2)}) collective-permute-start(f32[256,2]{0,1:T(2,128)S(1)} %slice.192), channel_id=1, source_target_pairs={{0,16},{16,32},{32,48},{48,64},{64,80},{80,96},{96,112},{1,17},{17... | collective-permute-start | bytes 6152 | tf_op jit(solution)/shard_map/ppermute | solution.py:18
  322.3 6.8 %collective-permute-start.2 = (f32[256,1]{0,1:T(1,128)S(1)}, f32[256,1]{0,1:T(1,128)S(1)}, u32[]{:S(2)}, u32[]{:S(2)}) collective-permute-start(f32[256,1]{0,1:T(1,128)S(1)} %slice.193), channel_id=1, source_target_pairs={{0,16},{16,32},{32,48},{48,64},{64,80},{80,96},{96,112},{1,17},{17... | collective-permute-start | bytes 3080 | tf_op jit(solution)/shard_map/ppermute | solution.py:28
  327.8 7.4 %collective-permute-start.3 = (f32[256,1]{0,1:T(1,128)S(1)}, f32[256,1]{0,1:T(1,128)S(1)}, u32[]{:S(2)}, u32[]{:S(2)}) collective-permute-start(f32[256,1]{0,1:T(1,128)S(1)} %slice.194), channel_id=1, source_target_pairs={{16,0},{32,16},{48,32},{64,48},{80,64},{96,80},{112,96},{17,1},{33... | collective-permute-start | bytes 3080 | tf_op jit(solution)/shard_map/ppermute | solution.py:29
  338.3 4.6 collective-permute-start.4
  339.8 4.1 collective-permute-start.5
  347.2 7.6 %collective-permute-start.6 = (f32[256,2]{0,1:T(2,128)S(1)}, f32[256,2]{0,1:T(2,128)S(1)}, u32[]{:S(2)}, u32[]{:S(2)}) collective-permute-start(f32[256,2]{0,1:T(2,128)S(1)} %get-tuple-element.138), channel_id=1, source_target_pairs={{0,16},{16,32},{32,48},{48,64},{64,80},{80,96},{96,112},{1,17},{17... | collective-permute-start | bytes 6152 | tf_op jit(solution)/shard_map/ppermute | solution.py:28
  353.5 7.0 %collective-permute-start.7 = (f32[256,2]{0,1:T(2,128)S(1)}, f32[256,2]{0,1:T(2,128)S(1)}, u32[]{:S(2)}, u32[]{:S(2)}) collective-permute-start(f32[256,2]{0,1:T(2,128)S(1)} %get-tuple-element.137), channel_id=1, source_target_pairs={{16,0},{32,16},{48,32},{64,48},{80,64},{96,80},{112,96},{17,1},{33... | collective-permute-start | bytes 6152 | tf_op jit(solution)/shard_map/ppermute | solution.py:29
  497.5 14.5 %all-to-all-start.1 = ((f32[8,64,1]{1,2,0:T(1,128)}), f32[8,64,1]{1,2,0:T(1,128)S(1)}, u32[]{:S(2)}, u32[]{:S(2)}) async-start(f32[8,64,1]{1,2,0:T(1,128)} %bitcast.14), calls=%async_computation.2 | async-start | bytes 8192 | tf_op jit(solution)/shard_map/all_to_all | solution.py:210
Sparse Core Ops, SparseCore 0:
  102.3 58.1 reduce-scatter.6
  216.8 93.3 reduce-scatter.4
  365.5 91.8 all-gather.1
where the time goes:
time: 522 us; the launch traced here: 521 us
  waiting for transfers between devices  269 us (52%)
  matrix products  78.1 us (15%)
  blocking collectives  51.9 us (10%)
  other arithmetic  47 us (9%)
  starting transfers between devices  39.8 us (8%)
  local copies, waits for them, and re-layouts  20.7 us (4%)
  between operations  14 us (3%)
    reduce_scatter x1, waiting for transfers between devices, on_device(): lax.psum_scatter(deposit_cycles(arrived, jnp.int32(0), CR * lax.axis_size...  93.5 us
    all_gather x1, waiting for transfers between devices, on_device(): lax.all_gather(widened, 'col', axis=0, tiled=True)  92 us
    unnamed x4, waiting for transfers between devices  57.9 us
    dot_general x1, matrix products, sample_field(): jnp.dot(field_part, axial_weights, precision=lax.Precision.HIGHEST, prefe...  39.4 us
    reduce_sum x4, other arithmetic, pair_sums(): jnp.sum(radial_part, axis=1)  39 us
    dot_general x1, matrix products, deposit_cycles(): lax.dot_general(radial_weights, axial_weights, (((1,), (1,)), ((), ())),...  37.6 us
    all_gather x1, blocking collectives, on_device(): lax.all_gather(own_sources, 'row', axis=1, tiled=True)  32.1 us
    all_gather x1, blocking collectives, on_device(): row_targets = lax.all_gather(positions, 'col', axis=1, tiled=True)  19.8 us
  transfers between devices with their start and end apart: 13, of which 7 were waited for; matrix products, arithmetic and copies ran while one was open for 1% of the time, Pallas kernels for 0%

commit v1 on v0

--- a/solution.py
+++ b/solution.py
@@ -1,3 +1,4 @@
+import functools
 import math
 import jax
 import jax.numpy as jnp
@@ -10,6 +11,14 @@
 CORE_SQUARE = 4.0
 STEP_LENGTH = 4.0
 VISCOSITY = 0.2
+
+
+def meet_leaf_all(array_in, ndim_at, dimension_no):
+    field_out = jnp.stack(jnp.split(array_in, lax.axis_size("row"), ndim_at), axis=0)
+    return jnp.concatenate(lax.all_to_all(field_out, "row", 0, 0), axis=dimension_no)
+
+
+play_the_levels_all = functools.partial(meet_leaf_all, ndim_at=1, dimension_no=1)
 
 
 def passed_along(block, axis, distance):
@@ -189,7 +198,7 @@
     outgoing = jnp.dot(
         payload, slot_table, precision=lax.Precision.HIGHEST, preferred_element_type=jnp.float32
     )
-    arrived = lax.all_to_all(outgoing, "row", split_axis=1, concat_axis=1, tiled=True)
+    arrived = play_the_levels_all(outgoing)
     folded_r = lax.psum_scatter(
         deposit_cycles(arrived, jnp.int32(0), CR * lax.axis_size("col"), col_start - 1, CZ + 3),
         "col",

time: 522 us -> 522 us (level)
  no operation moved by 1% of the time
where the time goes in v1:
time: 522 us; the launch traced here: 521 us
  waiting for transfers between devices  269 us (52%)
  matrix products  78.1 us (15%)
  blocking collectives  51.9 us (10%)
  other arithmetic  47 us (9%)
  starting transfers between devices  39.7 us (8%)
  local copies, waits for them, and re-layouts  20.9 us (4%)
  between operations  14 us (3%)
    reduce_scatter x1, waiting for transfers between devices, on_device(): lax.psum_scatter(deposit_cycles(arrived, jnp.int32(0), CR * lax.axis_size...  93.5 us
    all_gather x1, waiting for transfers between devices, on_device(): lax.all_gather(widened, 'col', axis=0, tiled=True)  92 us
    unnamed x4, waiting for transfers between devices  57.9 us
    dot_general x1, matrix products, sample_field(): jnp.dot(field_part, axial_weights, precision=lax.Precision.HIGHEST, prefe...  39.5 us
    reduce_sum x4, other arithmetic, pair_sums(): jnp.sum(radial_part, axis=1)  39 us
    dot_general x1, matrix products, deposit_cycles(): lax.dot_general(radial_weights, axial_weights, (((1,), (1,)), ((), ())),...  37.6 us
    all_gather x1, blocking collectives, on_device(): lax.all_gather(own_sources, 'row', axis=1, tiled=True)  32.1 us
    all_gather x1, blocking collectives, on_device(): row_targets = lax.all_gather(positions, 'col', axis=1, tiled=True)  19.8 us
  transfers between devices with their start and end apart: 13, of which 7 were waited for; matrix products, arithmetic and copies ran while one was open for 1% of the time, Pallas kernels for 0%

profile of v1, /device:TPU:0, one launch (start us, length us, event | category | flops | bytes accessed | tf_op | source)
XLA Modules:
  0.0 520.9 jit_solution(18301740788495701397)
XLA Ops:
  7.2 0.7 broadcast_in_dim.20
  8.1 0.8 slice_add_fusion.2
  8.9 0.7 pad_maximum_fusion.4
  9.6 32.1 %all_gather.9 = f32[3,1024]{1,0:T(4,128)S(1)} all-gather(f32[3,128]{1,0:T(4,128)S(1)} %pad_maximum_fusion.4), channel_id=1, replica_groups=mesh['row'=8,'col'=16] {'row'}, dimensions={1}, use_global_device_ids=true | all-gather | bytes 13824 | tf_op jit(solution)/shard_map/all_gather | solution.py:180
  41.6 19.8 %all_gather.10 = f32[2,2048]{1,0:T(2,128)S(1)} all-gather(f32[2,128]{1,0:T(2,128)S(1)} %pad_maximum_fusion.5), channel_id=1, replica_groups=mesh['row'=8,'col'=16] {'col'}, dimensions={1}, use_global_device_ids=true | all-gather | bytes 17408 | tf_op jit(solution)/shard_map/all_gather | solution.py:178
  61.5 39.3 %while.14 = (s32[]{:T(128)}, f32[4,2,512]{2,1,0:T(2,128)S(1)}, f32[3,1024]{1,0:T(4,128)S(1)}, f32[4,2,512]{2,1,0:T(2,128)S(1)}, f32[1,1024]{1,0:T(1,128)S(1)}, /*index=5*/s32[]{:T(128)}, s32[]{:T(128)}, s32[]{}) while((s32[]{:T(128)}, f32[4,2,512]{2,1,0:T(2,128)S(1)}, f32[3,1024]{1,0:T(4,128)S(1)}, f32[4,2,512]{2,1,0:T(2,128)S(1)}, ...), condition=%wide.region_3.4_spmd, body=%wide.region_0.3_spmd.sunk | while | flops 40895488 | bytes 75893 | solution.py:88
  61.5 9.7 %fusion.90 = (f32[512]{0:T(512)S(1)}, f32[512]{0:T(512)S(1)}) fusion(f32[512]{0:T(512)S(1)} %get-tuple-element.184, f32[1024]{0:T(1024)S(1)} %bitcast.92, f32[1024]{0:T(1024)S(1)} %bitcast.82, f32[512]{0:T(512)S(1)} %bitcast.90, f32[1024]{0:T(1024)S(1)} %bitcast.83, f32[512]{0:T(512)S(1)} %bitcast.80, f32[512]{0:T(512)S(1)} %get-tuple-element.188, ...), kind=kLoop, calls=%fused_computation.38.clone.1 | loop fusion | flops 40893440 | bytes 28672 | tf_op jit(solution)/shard_map/while/body/eval_jaxpr/reduce_sum | solution.py:81
  71.3 9.7 %fusion.90 = (f32[512]{0:T(512)S(1)}, f32[512]{0:T(512)S(1)}) fusion(f32[512]{0:T(512)S(1)} %get-tuple-element.184, f32[1024]{0:T(1024)S(1)} %bitcast.92, f32[1024]{0:T(1024)S(1)} %bitcast.82, f32[512]{0:T(512)S(1)} %bitcast.90, f32[1024]{0:T(1024)S(1)} %bitcast.83, f32[512]{0:T(512)S(1)} %bitcast.80, f32[512]{0:T(512)S(1)} %get-tuple-element.188, ...), kind=kLoop, calls=%fused_computation.38.clone.1 | loop fusion | flops 40893440 | bytes 28672 | tf_op jit(solution)/shard_map/while/body/eval_jaxpr/reduce_sum | solution.py:81
  81.2 9.7 %fusion.90 = (f32[512]{0:T(512)S(1)}, f32[512]{0:T(512)S(1)}) fusion(f32[512]{0:T(512)S(1)} %get-tuple-element.184, f32[1024]{0:T(1024)S(1)} %bitcast.92, f32[1024]{0:T(1024)S(1)} %bitcast.82, f32[512]{0:T(512)S(1)} %bitcast.90, f32[1024]{0:T(1024)S(1)} %bitcast.83, f32[512]{0:T(512)S(1)} %bitcast.80, f32[512]{0:T(512)S(1)} %get-tuple-element.188, ...), kind=kLoop, calls=%fused_computation.38.clone.1 | loop fusion | flops 40893440 | bytes 28672 | tf_op jit(solution)/shard_map/while/body/eval_jaxpr/reduce_sum | solution.py:81
  91.0 9.8 %fusion.90 = (f32[512]{0:T(512)S(1)}, f32[512]{0:T(512)S(1)}) fusion(f32[512]{0:T(512)S(1)} %get-tuple-element.184, f32[1024]{0:T(1024)S(1)} %bitcast.92, f32[1024]{0:T(1024)S(1)} %bitcast.82, f32[512]{0:T(512)S(1)} %bitcast.90, f32[1024]{0:T(1024)S(1)} %bitcast.83, f32[512]{0:T(512)S(1)} %bitcast.80, f32[512]{0:T(512)S(1)} %get-tuple-element.188, ...), kind=kLoop, calls=%fused_computation.38.clone.1 | loop fusion | flops 40893440 | bytes 28672 | tf_op jit(solution)/shard_map/while/body/eval_jaxpr/reduce_sum | solution.py:81
  100.8 1.3 copy.29
  102.7 57.9 %reduce-scatter.7.cloned.1.call-done = f32[128,2]{1,0:T(8,128)} async-done(((f32[2048,2]{1,0:T(8,128)}), f32[128,2]{1,0:T(8,128)}) %reduce-scatter.7.cloned.1.call-update) | async-done | bytes 1040
  160.6 0.9 copy.30
  162.6 0.7 reshape.310
  163.3 6.6 %all-to-all-start = ((f32[8,1,320]{2,1,0:T(1,128)}), f32[8,1,320]{2,1,0:T(1,128)S(1)}, u32[]{:S(2)}, u32[]{:S(2)}) async-start(f32[8,1,320]{2,1,0:T(1,128)} %reshape.310), calls=%async_computation | async-start | bytes 24576 | tf_op jit(solution)/shard_map/all_to_all | solution.py:18
  170.1 7.5 %all-to-all-done = f32[8,1,320]{2,1,0:T(1,128)S(1)} async-done(((f32[8,1,320]{2,1,0:T(1,128)}), f32[8,1,320]{2,1,0:T(1,128)S(1)}, u32[]{:S(2)}, u32[]{:S(2)}) %all-to-all-start) | async-done | bytes 10272 | tf_op jit(solution)/shard_map/all_to_all | solution.py:18
  178.1 0.7 reduce.34
  179.3 37.6 %fusion.25 = f32[4096,1027]{0,1:T(8,128)} fusion(f32[512]{0:T(512)S(1)} %mul.386, s32[512]{0:T(512)S(1)} %convert_element_type.62, f32[512]{0:T(512)S(1)} %sub.233, s32[512]{0:T(512)S(1)} %convert_element_type.65, s32[1027]{0:T(1024)S(1)} %iota_add_fusion.2, f32[512]{0:T(512)S(1)} %sub.241), kind=kOutput, calls=%fused_computation.45 | convolution fusion | flops 25863135232 | bytes 16840716 | tf_op jit(solution)/shard_map/dot_general | solution.py:141
  216.9 93.5 %reduce-scatter.5.cloned.1.call-done = f32[256,1027]{0,1:T(8,128)} async-done(((f32[4096,1027]{0,1:T(8,128)}), f32[256,1027]{0,1:T(8,128)}) %reduce-scatter.5.cloned.1.call-update) | async-done | bytes 1051664 | tf_op jit(solution)/shard_map/reduce_scatter | solution.py:202
  310.5 0.7 slice.190
  311.2 1.3 collective-permute-start
  313.1 0.7 slice.192
  313.8 6.0 %collective-permute-start.1 = (f32[256,2]{0,1:T(2,128)S(1)}, f32[256,2]{0,1:T(2,128)S(1)}, u32[]{:S(2)}, u32[]{:S(2)}) collective-permute-start(f32[256,2]{0,1:T(2,128)S(1)} %slice.192), channel_id=1, source_target_pairs={{0,16},{16,32},{32,48},{48,64},{64,80},{80,96},{96,112},{1,17},{17... | collective-permute-start | bytes 6152 | tf_op jit(solution)/shard_map/ppermute | solution.py:27
  319.8 1.3 slice.188
  321.1 0.7 slice_add_fusion
  322.6 5.5 %collective-permute-start.2 = (f32[256,1]{0,1:T(1,128)S(1)}, f32[256,1]{0,1:T(1,128)S(1)}, u32[]{:S(2)}, u32[]{:S(2)}) collective-permute-start(f32[256,1]{0,1:T(1,128)S(1)} %slice.193), channel_id=1, source_target_pairs={{0,16},{16,32},{32,48},{48,64},{64,80},{80,96},{96,112},{1,17},{17... | collective-permute-start | bytes 3080 | tf_op jit(solution)/shard_map/ppermute | solution.py:37
  328.1 1.3 collective-permute-start.3
  329.4 6.1 %collective-permute-done.3 = f32[256,1]{0,1:T(1,128)S(1)} collective-permute-done((f32[256,1]{0,1:T(1,128)S(1)}, f32[256,1]{0,1:T(1,128)S(1)}, u32[]{:S(2)}, u32[]{:S(2)}) %collective-permute-start.3) | collective-permute-done | bytes 1056 | tf_op jit(solution)/shard_map/ppermute | solution.py:38
  335.4 0.9 concatenate.28
  336.3 0.9 fusion.82
  337.3 1.2 copy.23
  338.5 1.3 collective-permute-start.4
  340.0 3.0 collective-permute-start.5
  343.1 1.0 copy.24
  344.2 1.0 copy.26
  345.2 2.2 fusion.59
  347.4 6.3 %collective-permute-start.6 = (f32[256,2]{0,1:T(2,128)S(1)}, f32[256,2]{0,1:T(2,128)S(1)}, u32[]{:S(2)}, u32[]{:S(2)}) collective-permute-start(f32[256,2]{0,1:T(2,128)S(1)} %get-tuple-element.138), channel_id=1, source_target_pairs={{0,16},{16,32},{32,48},{48,64},{64,80},{80,96},{96,112},{1,17},{17... | collective-permute-start | bytes 6152 | tf_op jit(solution)/shard_map/ppermute | solution.py:37
  353.7 1.3 collective-permute-start.7
  355.0 5.7 %collective-permute-done.7 = f32[256,2]{0,1:T(2,128)S(1)} collective-permute-done((f32[256,2]{0,1:T(2,128)S(1)}, f32[256,2]{0,1:T(2,128)S(1)}, u32[]{:S(2)}, u32[]{:S(2)}) %collective-permute-start.7) | collective-permute-done | bytes 2080 | tf_op jit(solution)/shard_map/ppermute | solution.py:38
  360.7 4.9 concatenate.33
  365.6 92.0 %all-gather.2.cloned.1.call-done = f32[4096,1028]{0,1:T(8,128)} async-done(((f32[256,1028]{0,1:T(8,128)}), f32[4096,1028]{0,1:T(8,128)}) %all-gather.2.cloned.1.call-update) | async-done | bytes 16842768 | tf_op jit(solution)/shard_map/all_gather | solution.py:217
  457.6 39.5 %multiply_reduce_fusion = f32[512]{0:T(512)S(1)} fusion(f32[4096,1028]{0,1:T(8,128)} %all-gather.2.cloned.1.call-done, s32[512]{0:T(512)S(1)} %convert_element_type.62, f32[512]{0:T(512)S(1)} %sub.233, s32[512]{0:T(512)S(1)} %convert_element_type.65, s32[1028]{0:T(1024)S(1)} %iota_add_fusion.1, f32[512]{0:T(512)S(1)} %sub.241), kind=kOutput, calls=%fused_computation.44 | convolution fusion | flops 25890402304 | bytes 16857104 | tf_op jit(solution)/shard_map/dot_general | solution.py:155
  497.1 0.7 all_to_all.12
  497.8 6.8 %all-to-all-start.1 = ((f32[8,64,1]{1,2,0:T(1,128)}), f32[8,64,1]{1,2,0:T(1,128)S(1)}, u32[]{:S(2)}, u32[]{:S(2)}) async-start(f32[8,64,1]{1,2,0:T(1,128)} %bitcast.23), calls=%async_computation.2 | async-start | bytes 8192 | tf_op jit(solution)/shard_map/all_to_all | solution.py:219
  504.6 1.3 copy.28
  505.9 6.4 %all-to-all-done.1 = f32[8,64,1]{1,2,0:T(1,128)S(1)} async-done(((f32[8,64,1]{1,2,0:T(1,128)}), f32[8,64,1]{1,2,0:T(1,128)S(1)}, u32[]{:S(2)}, u32[]{:S(2)}) %all-to-all-start.1) | async-done | bytes 2080 | tf_op jit(solution)/shard_map/all_to_all | solution.py:219
  512.8 0.7 reduce.33
  513.5 0.8 convolution_bitcast_fusion
  (74 shorter events, 5.4 us)
Async XLA Ops:
  7.2 153.4 %reduce-scatter.7.cloned.1.call-start = ((), (), s32[]{:S(2)}) async-start(), calls=%async_computation.6 | async-start | bytes 1114112
  100.8 1.4 copy-start.1
  100.8 60.6 %copy-start = (f32[2,128]{1,0:T(2,128)S(1)}, f32[2,128]{1,0:T(2,128)}, u32[]{:S(2)}) copy-start(f32[2,128]{1,0:T(2,128)} %param.11) | copy-start | bytes 3076
  100.8 61.2 %copy-start.2 = (f32[128]{0:T(128)S(1)}, f32[128]{0:T(128)}, u32[]{:S(2)}) copy-start(f32[128]{0:T(128)} %param.12) | copy-start | bytes 1540
  163.3 14.3 %all-to-all-start = ((f32[8,1,320]{2,1,0:T(1,128)}), f32[8,1,320]{2,1,0:T(1,128)S(1)}, u32[]{:S(2)}, u32[]{:S(2)}) async-start(f32[8,1,320]{2,1,0:T(1,128)} %reshape.310), calls=%async_computation | async-start | bytes 24576 | tf_op jit(solution)/shard_map/all_to_all | solution.py:18
  169.8 140.6 %reduce-scatter.5.cloned.1.call-start = ((), (), s32[]{:S(2)}) async-start(), calls=%async_computation.4 | async-start | bytes 17965056 | tf_op jit(solution)/shard_map/reduce_scatter | solution.py:202
  216.9 240.7 %all-gather.2.cloned.1.call-start = ((), (), s32[]{:S(2)}) async-start(), calls=%async_computation.5 | async-start | bytes 17965056 | tf_op jit(solution)/shard_map/all_gather | solution.py:217
  311.2 10.0 %collective-permute-start = (f32[256,1]{0,1:T(1,128)S(1)}, f32[256,1]{0,1:T(1,128)S(1)}, u32[]{:S(2)}, u32[]{:S(2)}) collective-permute-start(f32[256,1]{0,1:T(1,128)S(1)} %slice.190), channel_id=1, source_target_pairs={{16,0},{32,16},{48,32},{64,48},{80,64},{96,80},{112,96},{17,1},{33... | collective-permute-start | bytes 3080 | tf_op jit(solution)/shard_map/ppermute | solution.py:27
  313.8 8.1 %collective-permute-start.1 = (f32[256,2]{0,1:T(2,128)S(1)}, f32[256,2]{0,1:T(2,128)S(1)}, u32[]{:S(2)}, u32[]{:S(2)}) collective-permute-start(f32[256,2]{0,1:T(2,128)S(1)} %slice.192), channel_id=1, source_target_pairs={{0,16},{16,32},{32,48},{48,64},{64,80},{80,96},{96,112},{1,17},{17... | collective-permute-start | bytes 6152 | tf_op jit(solution)/shard_map/ppermute | solution.py:27
  322.6 6.8 %collective-permute-start.2 = (f32[256,1]{0,1:T(1,128)S(1)}, f32[256,1]{0,1:T(1,128)S(1)}, u32[]{:S(2)}, u32[]{:S(2)}) collective-permute-start(f32[256,1]{0,1:T(1,128)S(1)} %slice.193), channel_id=1, source_target_pairs={{0,16},{16,32},{32,48},{48,64},{64,80},{80,96},{96,112},{1,17},{17... | collective-permute-start | bytes 3080 | tf_op jit(solution)/shard_map/ppermute | solution.py:37
  328.1 7.4 %collective-permute-start.3 = (f32[256,1]{0,1:T(1,128)S(1)}, f32[256,1]{0,1:T(1,128)S(1)}, u32[]{:S(2)}, u32[]{:S(2)}) collective-permute-start(f32[256,1]{0,1:T(1,128)S(1)} %slice.194), channel_id=1, source_target_pairs={{16,0},{32,16},{48,32},{64,48},{80,64},{96,80},{112,96},{17,1},{33... | collective-permute-start | bytes 3080 | tf_op jit(solution)/shard_map/ppermute | solution.py:38
  338.5 4.6 collective-permute-start.4
  340.0 4.1 collective-permute-start.5
  347.4 7.6 %collective-permute-start.6 = (f32[256,2]{0,1:T(2,128)S(1)}, f32[256,2]{0,1:T(2,128)S(1)}, u32[]{:S(2)}, u32[]{:S(2)}) collective-permute-start(f32[256,2]{0,1:T(2,128)S(1)} %get-tuple-element.138), channel_id=1, source_target_pairs={{0,16},{16,32},{32,48},{48,64},{64,80},{80,96},{96,112},{1,17},{17... | collective-permute-start | bytes 6152 | tf_op jit(solution)/shard_map/ppermute | solution.py:37
  353.7 7.0 %collective-permute-start.7 = (f32[256,2]{0,1:T(2,128)S(1)}, f32[256,2]{0,1:T(2,128)S(1)}, u32[]{:S(2)}, u32[]{:S(2)}) collective-permute-start(f32[256,2]{0,1:T(2,128)S(1)} %get-tuple-element.137), channel_id=1, source_target_pairs={{16,0},{32,16},{48,32},{64,48},{80,64},{96,80},{112,96},{17,1},{33... | collective-permute-start | bytes 6152 | tf_op jit(solution)/shard_map/ppermute | solution.py:38
  497.8 14.5 %all-to-all-start.1 = ((f32[8,64,1]{1,2,0:T(1,128)}), f32[8,64,1]{1,2,0:T(1,128)S(1)}, u32[]{:S(2)}, u32[]{:S(2)}) async-start(f32[8,64,1]{1,2,0:T(1,128)} %bitcast.23), calls=%async_computation.2 | async-start | bytes 8192 | tf_op jit(solution)/shard_map/all_to_all | solution.py:219
Sparse Core Ops, SparseCore 0:
  102.3 58.1 reduce-scatter.6
  217.0 93.4 reduce-scatter.4
  365.7 91.8 all-gather.1
